TPU v7x, 1024 devices: a whole 8x8x8 slice. The times are simulated.
1024 devices in a mesh: row: 64 (over z, x), col: 16 (over y, core).
Axes of the slice: x: 8, y: 8, z: 8, core: 2. Of those that a mesh axis runs over, the one named last changes fastest.
Arguments:
- a_tiles: bfloat16 [256, 48, 5, 128, 128], P('row', 'col'), may hold values from -0.25 to 0.25
- p_tiles: bfloat16 [256, 48, 2, 128, 128], P('row', 'col'), may hold values from -0.5 to 0.5
- c_slot: int32 [256, 48, 2, 5, 2], P('row', 'col'), may hold values from 0 to 95, as said below
Outputs:
- coarse: float32 [6144, 128, 128], P(('row', 'col'))
Inputs may be any that keep to these rules, and one draw needn't show every extreme that they name: `c_slot`: each tile of a fine block belongs to an aggregate I of its grid row of devices, owned by owner I // 2, where owner o holds coarse tiles o * 6 to (o + 1) * 6 - 1. A term's label is owner(I) * 6 + 3 (I mod 2) + 0, 1 or 2, as the aggregate J of the neighbour tile is I itself, another aggregate of the same owner, or an aggregate of another owner (outside the grid J is I). The tiles of fine blocks on device column j belong to aggregates of owners j - 1, j or j + 1 only, so a device's terms land only in tiles of those owners.
All inputs are finite; a program needn't handle non-finite values.
Results may differ from a plain program's by a relative error of at most 0.0029.
Values may be sent and summed in bfloat16 or wider, within the bound.
A program may use at most 128 MiB of HBM per device.

v0:
```python
import jax
import jax.numpy as jnp
from jax import lax
from jax.sharding import PartitionSpec as P

CTD = 6


def padded_2(cells, sides, width):
    for axis, dim in sides:
        count = lax.axis_size(axis)
        ends = count - 1
        head = lax.slice_in_dim(cells, 0, width, axis=dim)
        tail = lax.slice_in_dim(cells, cells.shape[dim] - width, cells.shape[dim], axis=dim)
        cells = jnp.concatenate(
            [
                lax.ppermute(tail, axis, [(i, (i + 1) % count) for i in range(ends)]),
                cells,
                lax.ppermute(head, axis, [((i + 1) % count, i) for i in range(ends)]),
            ],
            axis=dim,
        )
    return cells


def shifted(block, axis, distance):
    devices = range(lax.axis_size(axis))
    route = [(i - distance, i) for i in devices if i - distance in devices]
    return lax.ppermute(block, axis, route)


def body(a_tiles, p_tiles, c_slot):
    tile = p_tiles.shape[-1]
    padded = padded_2(p_tiles, (("row", 0), ("col", 1)), 1)
    own = padded[1:-1, 1:-1]
    near = jnp.stack(
        [own, padded[:-2, 1:-1], padded[2:, 1:-1], padded[1:-1, :-2], padded[1:-1, 2:]], axis=2
    )
    ap_tiles = jnp.einsum(
        "xykij,xykqjl->xykqil", a_tiles, near, preferred_element_type=jnp.float32
    ).astype(jnp.bfloat16)
    terms = jnp.einsum("xypji,xykqjl->xypkqil", own, ap_tiles, preferred_element_type=jnp.float32)
    count = terms.shape[0] * terms.shape[1] * terms.shape[2] * terms.shape[3] * terms.shape[4]
    term_flat = terms.reshape(count, tile * tile)
    column = lax.axis_index("col")
    local_label = c_slot.reshape(count) - (column - 1) * CTD
    slot_ids = jnp.arange(3 * CTD, dtype=jnp.int32)
    one_hot = (local_label[:, None] == slot_ids[None, :]).astype(jnp.float32)
    summed = jnp.dot(
        one_hot.T, term_flat, precision=lax.Precision.HIGHEST, preferred_element_type=jnp.float32
    )
    summed = summed.reshape(3 * CTD, tile, tile)
    lower_part = summed[:CTD]
    mine = summed[CTD : 2 * CTD]
    upper_part = summed[2 * CTD :]
    from_lower = shifted(upper_part, "col", 1)
    from_upper = shifted(lower_part, "col", -1)
    coarse = mine + from_lower + from_upper
    return coarse


def solution(mesh):
    in_specs = (
        P("row", "col", None, None, None),
        P("row", "col", None, None, None),
        P("row", "col", None, None, None),
    )
    out_specs = P(("row", "col"), None, None)
    return jax.shard_map(body, mesh=mesh, in_specs=in_specs, out_specs=out_specs, check_vma=False)
```

profile of v0, /device:TPU:447, one launch (start us, length us, event | category | flops | bytes accessed | tf_op | source)
XLA Modules:
  0.0 99.8 jit_solution(5438250500286240187)
XLA Ops:
  0.0 0.0 copy-start
  0.0 0.0 copy-start.1
  0.0 1.2 %fusion.28 = (bf16[1,3,2,128,128]{4,3,2,1,0:T(8,128)(2,1)S(1)}, bf16[1,3,2,128,128]{4,3,2,1,0:T(8,128)(2,1)S(1)}) fusion(bf16[4,3,2,128,128]{4,3,2,1,0:T(8,128)(2,1)} %param.4), kind=kLoop, calls=%fused_computation.37 | loop fusion | bytes 786432 | tf_op jit(solution)/shard_map/slice | solution.py:13
  1.2 5.9 %collective-permute-start = (bf16[1,3,2,128,128]{4,3,2,1,0:T(8,128)(2,1)S(1)}, bf16[1,3,2,128,128]{4,3,2,1,0:T(8,128)(2,1)S(1)}, u32[]{:S(2)}, u32[]{:S(2)}) collective-permute-start(bf16[1,3,2,128,128]{4,3,2,1,0:T(8,128)(2,1)S(1)} %get-tuple-element.11), channel_id=1, source_target_pairs={{0,16},{16,32},{32,48},{48,64},{64,80},{80,96},{96,112},{112,128},... | collective-permute-start | bytes 589832 | tf_op jit(solution)/shard_map/ppermute | solution.py:17
  7.1 1.9 %collective-permute-start.1 = (bf16[1,3,2,128,128]{4,3,2,1,0:T(8,128)(2,1)S(1)}, bf16[1,3,2,128,128]{4,3,2,1,0:T(8,128)(2,1)S(1)}, u32[]{:S(2)}, u32[]{:S(2)}) collective-permute-start(bf16[1,3,2,128,128]{4,3,2,1,0:T(8,128)(2,1)S(1)} %get-tuple-element.10), channel_id=1, source_target_pairs={{16,0},{32,16},{48,32},{64,48},{80,64},{96,80},{112,96},{128,112},... | collective-permute-start | bytes 589832 | tf_op jit(solution)/shard_map/ppermute | solution.py:19
  9.1 2.1 %bitcast_dynamic-update-slice_fusion = bf16[4,3,5,2,128,128]{5,4,3,1,0,2:T(8,128)(2,1)} fusion(bf16[4,3,2,128,128]{4,3,2,1,0:T(8,128)(2,1)} %param.4), kind=kLoop, calls=%fused_computation.22 | loop fusion | bytes 1572864
  11.2 0.0 copy-start.4
  11.2 0.0 collective-permute-done
  11.2 0.0 copy-done.1
  11.2 0.1 constant_dynamic-update-slice_fusion.1
  11.4 6.4 %collective-permute-done.1 = bf16[1,3,2,128,128]{4,3,2,1,0:T(8,128)(2,1)S(1)} collective-permute-done((bf16[1,3,2,128,128]{4,3,2,1,0:T(8,128)(2,1)S(1)}, bf16[1,3,2,128,128]{4,3,2,1,0:T(8,128)(2,1)S(1)}, u32[]{:S(2)}, u32[]{:S(2)}) %collective-permute-start.1) | collective-permute-done | bytes 196640 | tf_op jit(solution)/shard_map/ppermute | solution.py:19
  17.8 0.0 copy-start.2
  17.8 1.0 %copy-done.2 = bf16[6,3,2,128,128]{4,3,2,1,0:T(8,128)(2,1)} copy-done((bf16[6,3,2,128,128]{4,3,2,1,0:T(8,128)(2,1)}, bf16[6,3,2,128,128]{4,3,2,1,0:T(8,128)(2,1)S(1)}, u32[]{:S(2)}) %copy-start.2) | copy-done | bytes 1179672
  18.9 1.0 fusion.27
  19.8 6.3 %collective-permute-start.2 = (bf16[6,1,2,128,128]{4,3,2,1,0:T(8,128)(2,1)}, bf16[6,1,2,128,128]{4,3,2,1,0:T(8,128)(2,1)S(1)}, u32[]{:S(2)}, u32[]{:S(2)}) collective-permute-start(bf16[6,1,2,128,128]{4,3,2,1,0:T(8,128)(2,1)} %get-tuple-element.9), channel_id=1, source_target_pairs={{0,1},{1,2},{2,3},{3,4},{4,5},{5,6},{6,7},{7,8},{8,9},{9,10},{10,1... | collective-permute-start | bytes 1179656 | tf_op jit(solution)/shard_map/ppermute | solution.py:17
  26.1 0.0 copy-done.4
  26.1 0.6 broadcast_subtract_fusion
  26.7 1.6 %copy.4 = s32[4,3,2,5,2]{4,3,2,1,0:T(8,128)} copy(s32[4,3,2,5,2]{3,4,2,1,0:T(2,128)} %broadcast_subtract_fusion) | data formatting | bytes 1920 | tf_op jit(solution)/shard_map/sub | solution.py:46
  28.3 1.0 %sub.19 = s32[240]{0:T(256)S(1)} reshape(s32[4,3,2,5,2]{4,3,2,1,0:T(8,128)} %copy.4) | data formatting | bytes 1920 | tf_op jit(solution)/shard_map/sub | solution.py:46
  29.4 0.0 copy-start.3
  29.4 2.1 %collective-permute-start.3 = (bf16[6,1,2,128,128]{4,3,2,1,0:T(8,128)(2,1)}, bf16[6,1,2,128,128]{4,3,2,1,0:T(8,128)(2,1)S(1)}, u32[]{:S(2)}, u32[]{:S(2)}) collective-permute-start(bf16[6,1,2,128,128]{4,3,2,1,0:T(8,128)(2,1)} %get-tuple-element.8), channel_id=1, source_target_pairs={{1,0},{2,1},{3,2},{4,3},{5,4},{6,5},{7,6},{8,7},{9,8},{10,9},{11,1... | collective-permute-start | bytes 1179656 | tf_op jit(solution)/shard_map/ppermute | solution.py:19
  31.4 1.0 fusion.15
  32.4 1.0 fusion.13
  33.4 0.0 collective-permute-done.2
  33.4 0.0 copy-done.3
  33.4 0.9 fusion.11
  34.3 5.7 %collective-permute-done.3 = bf16[6,1,2,128,128]{4,3,2,1,0:T(8,128)(2,1)S(1)} collective-permute-done((bf16[6,1,2,128,128]{4,3,2,1,0:T(8,128)(2,1)}, bf16[6,1,2,128,128]{4,3,2,1,0:T(8,128)(2,1)S(1)}, u32[]{:S(2)}, u32[]{:S(2)}) %collective-permute-start.3) | collective-permute-done | bytes 393248 | tf_op jit(solution)/shard_map/ppermute | solution.py:19
  40.0 0.9 fusion.9
  41.0 0.0 copy-done
  41.0 10.9 %convolution_bitcast_fusion = f32[4,3,2,5,2,128,128]{5,6,2,4,3,1,0:T(8,128)} fusion(bf16[4,3,2,128,128]{4,3,2,1,0:T(8,128)(2,1)S(1)} %copy-done.1, bf16[4,3,5,2,128,128]{5,4,3,1,0,2:T(8,128)(2,1)} %fusion.9, bf16[4,3,5,128,128]{4,3,2,1,0:T(8,128)(2,1)S(1)} %copy-done), kind=kOutput, calls=%fused_computation.3 | convolution fusion | flops 1511915520 | bytes 22413312 | tf_op jit(solution)/shard_map/xypji,xykqjl->xypkqil/dot_general | solution.py:42
  51.9 15.7 %copy.5 = f32[4,3,2,5,2,128,128]{6,5,4,3,2,1,0:T(8,128)} copy(f32[4,3,2,5,2,128,128]{5,6,2,4,3,1,0:T(8,128)} %convolution_bitcast_fusion) | data formatting | bytes 31457280 | tf_op jit(solution)/shard_map/xypji,xykqjl->xypkqil/transpose | solution.py:42
  67.6 18.9 %fusion = f32[18,16384]{1,0:T(8,128)S(1)} fusion(f32[30,8,128,128]{3,2,1,0:T(8,128)} %bitcast.62, s32[240]{0:T(256)S(1)} %sub.19), kind=kOutput, calls=%fused_computation | convolution fusion | flops 849350912 | bytes 16909248 | tf_op jit(solution)/shard_map/dot_general | solution.py:49
  86.5 0.1 slice_bitcast_fusion.2
  86.6 0.1 copy.28
  86.7 1.9 %collective-permute-start.4 = (f32[6,128,128]{2,1,0:T(8,128)S(1)}, f32[6,128,128]{2,1,0:T(8,128)S(1)}, u32[]{:S(2)}, u32[]{:S(2)}) collective-permute-start(f32[6,128,128]{2,1,0:T(8,128)S(1)} %bitcast.63), channel_id=1, source_target_pairs={{0,1},{1,2},{2,3},{3,4},{4,5},{5,6},{6,7},{7,8},{8,9},{9,10},{10,1... | collective-permute-start | bytes 1179656 | tf_op jit(solution)/shard_map/ppermute | solution.py:29
  88.6 0.1 copy.27
  88.7 2.4 %collective-permute-start.5 = (f32[6,128,128]{2,1,0:T(8,128)S(1)}, f32[6,128,128]{2,1,0:T(8,128)S(1)}, u32[]{:S(2)}, u32[]{:S(2)}) collective-permute-start(f32[6,128,128]{2,1,0:T(8,128)S(1)} %bitcast.64), channel_id=1, source_target_pairs={{1,0},{2,1},{3,2},{4,3},{5,4},{6,5},{7,6},{8,7},{9,8},{10,9},{11,1... | collective-permute-start | bytes 1179656 | tf_op jit(solution)/shard_map/ppermute | solution.py:29
  91.1 2.2 %collective-permute-done.4 = f32[6,128,128]{2,1,0:T(8,128)S(1)} collective-permute-done((f32[6,128,128]{2,1,0:T(8,128)S(1)}, f32[6,128,128]{2,1,0:T(8,128)S(1)}, u32[]{:S(2)}, u32[]{:S(2)}) %collective-permute-start.4) | collective-permute-done | bytes 393248 | tf_op jit(solution)/shard_map/ppermute | solution.py:29
  93.3 5.7 %collective-permute-done.5 = f32[6,128,128]{2,1,0:T(8,128)S(1)} collective-permute-done((f32[6,128,128]{2,1,0:T(8,128)S(1)}, f32[6,128,128]{2,1,0:T(8,128)S(1)}, u32[]{:S(2)}, u32[]{:S(2)}) %collective-permute-start.5) | collective-permute-done | bytes 393248 | tf_op jit(solution)/shard_map/ppermute | solution.py:29
  99.0 0.8 fusion.25
  (2 shorter events, 0.0 us)
Async XLA Ops:
  0.0 41.0 %copy-start = (bf16[4,3,5,128,128]{4,3,2,1,0:T(8,128)(2,1)S(1)}, bf16[4,3,5,128,128]{4,3,2,1,0:T(8,128)(2,1)}, u32[]{:S(2)}) copy-start(bf16[4,3,5,128,128]{4,3,2,1,0:T(8,128)(2,1)} %param.3) | copy-start | bytes 5898244
  0.0 11.2 %copy-start.1 = (bf16[4,3,2,128,128]{4,3,2,1,0:T(8,128)(2,1)S(1)}, bf16[4,3,2,128,128]{4,3,2,1,0:T(8,128)(2,1)}, u32[]{:S(2)}) copy-start(bf16[4,3,2,128,128]{4,3,2,1,0:T(8,128)(2,1)} %param.4) | copy-start | bytes 2359300
  1.2 10.0 %collective-permute-start = (bf16[1,3,2,128,128]{4,3,2,1,0:T(8,128)(2,1)S(1)}, bf16[1,3,2,128,128]{4,3,2,1,0:T(8,128)(2,1)S(1)}, u32[]{:S(2)}, u32[]{:S(2)}) collective-permute-start(bf16[1,3,2,128,128]{4,3,2,1,0:T(8,128)(2,1)S(1)} %get-tuple-element.11), channel_id=1, source_target_pairs={{0,16},{16,32},{32,48},{48,64},{64,80},{80,96},{96,112},{112,128},... | collective-permute-start | bytes 589832 | tf_op jit(solution)/shard_map/ppermute | solution.py:17
  7.1 10.7 %collective-permute-start.1 = (bf16[1,3,2,128,128]{4,3,2,1,0:T(8,128)(2,1)S(1)}, bf16[1,3,2,128,128]{4,3,2,1,0:T(8,128)(2,1)S(1)}, u32[]{:S(2)}, u32[]{:S(2)}) collective-permute-start(bf16[1,3,2,128,128]{4,3,2,1,0:T(8,128)(2,1)S(1)} %get-tuple-element.10), channel_id=1, source_target_pairs={{16,0},{32,16},{48,32},{64,48},{80,64},{96,80},{112,96},{128,112},... | collective-permute-start | bytes 589832 | tf_op jit(solution)/shard_map/ppermute | solution.py:19
  11.2 14.9 %copy-start.4 = (s32[4,3,2,5,2]{3,4,2,1,0:T(2,128)S(1)}, s32[4,3,2,5,2]{3,4,2,1,0:T(2,128)}, u32[]{:S(2)}) copy-start(s32[4,3,2,5,2]{3,4,2,1,0:T(2,128)} %param.5) | copy-start | bytes 2884
  17.8 1.0 %copy-start.2 = (bf16[6,3,2,128,128]{4,3,2,1,0:T(8,128)(2,1)}, bf16[6,3,2,128,128]{4,3,2,1,0:T(8,128)(2,1)S(1)}, u32[]{:S(2)}) copy-start(bf16[6,3,2,128,128]{4,3,2,1,0:T(8,128)(2,1)S(1)} %constant_dynamic-update-slice_fusion) | copy-start | bytes 3538948
  19.8 13.5 %collective-permute-start.2 = (bf16[6,1,2,128,128]{4,3,2,1,0:T(8,128)(2,1)}, bf16[6,1,2,128,128]{4,3,2,1,0:T(8,128)(2,1)S(1)}, u32[]{:S(2)}, u32[]{:S(2)}) collective-permute-start(bf16[6,1,2,128,128]{4,3,2,1,0:T(8,128)(2,1)} %get-tuple-element.9), channel_id=1, source_target_pairs={{0,1},{1,2},{2,3},{3,4},{4,5},{5,6},{6,7},{7,8},{8,9},{9,10},{10,1... | collective-permute-start | bytes 1179656 | tf_op jit(solution)/shard_map/ppermute | solution.py:17
  29.4 4.0 %copy-start.3 = (bf16[6,3,2,128,128]{4,3,2,1,0:T(8,128)(2,1)S(1)}, bf16[6,3,2,128,128]{4,3,2,1,0:T(8,128)(2,1)}, u32[]{:S(2)}) copy-start(bf16[6,3,2,128,128]{4,3,2,1,0:T(8,128)(2,1)} %copy-done.2) | copy-start | bytes 3538948
  29.4 10.6 %collective-permute-start.3 = (bf16[6,1,2,128,128]{4,3,2,1,0:T(8,128)(2,1)}, bf16[6,1,2,128,128]{4,3,2,1,0:T(8,128)(2,1)S(1)}, u32[]{:S(2)}, u32[]{:S(2)}) collective-permute-start(bf16[6,1,2,128,128]{4,3,2,1,0:T(8,128)(2,1)} %get-tuple-element.8), channel_id=1, source_target_pairs={{1,0},{2,1},{3,2},{4,3},{5,4},{6,5},{7,6},{8,7},{9,8},{10,9},{11,1... | collective-permute-start | bytes 1179656 | tf_op jit(solution)/shard_map/ppermute | solution.py:19
  86.7 6.6 %collective-permute-start.4 = (f32[6,128,128]{2,1,0:T(8,128)S(1)}, f32[6,128,128]{2,1,0:T(8,128)S(1)}, u32[]{:S(2)}, u32[]{:S(2)}) collective-permute-start(f32[6,128,128]{2,1,0:T(8,128)S(1)} %bitcast.63), channel_id=1, source_target_pairs={{0,1},{1,2},{2,3},{3,4},{4,5},{5,6},{6,7},{7,8},{8,9},{9,10},{10,1... | collective-permute-start | bytes 1179656 | tf_op jit(solution)/shard_map/ppermute | solution.py:29
  88.7 10.3 %collective-permute-start.5 = (f32[6,128,128]{2,1,0:T(8,128)S(1)}, f32[6,128,128]{2,1,0:T(8,128)S(1)}, u32[]{:S(2)}, u32[]{:S(2)}) collective-permute-start(f32[6,128,128]{2,1,0:T(8,128)S(1)} %bitcast.64), channel_id=1, source_target_pairs={{1,0},{2,1},{3,2},{4,3},{5,4},{6,5},{7,6},{8,7},{9,8},{10,9},{11,1... | collective-permute-start | bytes 1179656 | tf_op jit(solution)/shard_map/ppermute | solution.py:29
where the time goes:
time: 100 us; the launch traced here: 99.8 us
  matrix products  29.8 us (30%)
  local copies, waits for them, and re-layouts  24.1 us (24%)
  starting transfers between devices  20.5 us (20%)
  waiting for transfers between devices  20 us (20%)
  other arithmetic  5.27 us (5%)
    dot_general x1, matrix products, body(): jnp.dot(one_hot.T, term_flat, precision=lax.Precision.HIGHEST, preferred_...  18.9 us
    transpose x1, local copies, waits for them, and re-layouts, body(): jnp.einsum('xypji,xykqjl->xypkqil', own, ap_tiles, preferred_element_type...  15.7 us
    ppermute x2, starting transfers between devices, padded_2(): lax.ppermute(tail, axis, [(i, (i + 1) % count) for i in range(ends)])  12.2 us
    ppermute x2, waiting for transfers between devices, padded_2(): lax.ppermute(head, axis, [((i + 1) % count, i) for i in range(ends)])  12.1 us
    dot_general x1, matrix products, body(): jnp.einsum('xypji,xykqjl->xypkqil', own, ap_tiles, preferred_element_type...  10.9 us
    ppermute x2, waiting for transfers between devices, shifted(): return lax.ppermute(block, axis, route)  7.89 us
    ppermute x2, starting transfers between devices, shifted(): return lax.ppermute(block, axis, route)  4.33 us
    ppermute x2, starting transfers between devices, padded_2(): lax.ppermute(head, axis, [((i + 1) % count, i) for i in range(ends)])  3.97 us
  transfers between devices with their start and end apart: 6, of which 4 were waited for; matrix products, arithmetic and copies ran while one was open for 8% of the time, Pallas kernels for 0%

commit v1 on v0

v1 whole, which is shorter than its diff:
```python
import functools

import jax
import jax.numpy as jnp
from jax import lax
from jax.experimental import pallas as pl
from jax.experimental.pallas import tpu as pltpu
from jax.sharding import PartitionSpec as P

MESH = pl.DeviceIdType.MESH
B = 128
KP = 2
FBR = 4
FBC = 3
CTD = 6
SELF, ABOVE, BELOW, LEFT, RIGHT = range(5)
F32, BF16 = jnp.float32, jnp.bfloat16


def place(r):
    return {1: (0, 0), 2: (0, 1), 0: (1, 0), 3: (1, 1)}[r]


def kernel(n_row, n_col, a_hbm, p_hbm, slot_hbm, mine_hbm, far_hbm, near_hbm, slot, a_v, p_v, acc, pt, g, part, mine_v, out_v,
           load_sem, halo_send, halo_recv, part_send, part_recv, store_sem):
    row, col = lax.axis_index("row"), lax.axis_index("col")
    odd = lax.rem(col, 2)
    far, near = col - 1 + 2 * odd, col + 1 - 2 * odd
    has_above, has_below = row > 0, row < n_row - 1
    has_far = jnp.logical_and(far >= 0, far < n_col)
    to_far, to_near = 2 * odd - 1, 1 - 2 * odd

    barrier = pltpu.get_barrier_semaphore()

    def greet(there):
        pl.semaphore_signal(barrier, inc=1, device_id=there, device_id_type=MESH)

    pl.when(has_above)(lambda: greet((row - 1, col)))
    pl.when(has_below)(lambda: greet((row + 1, col)))
    pl.when(has_far)(lambda: greet((row, far)))
    greet((row, near))

    load_p = pltpu.make_async_copy(p_hbm, p_v.at[pl.ds(1, FBR), pl.ds(1, FBC)], load_sem.at[0])
    load_a = pltpu.make_async_copy(a_hbm, a_v, load_sem.at[1])
    load_slot = pltpu.make_async_copy(slot_hbm, slot, load_sem.at[2])
    load_p.start()
    load_slot.start()
    load_a.start()

    def halo(index, source, target, there):
        return pltpu.make_async_remote_copy(
            src_ref=source, dst_ref=target, send_sem=halo_send.at[index], recv_sem=halo_recv.at[index],
            device_id=there, device_id_type=MESH)

    rim_above = p_v.at[0, pl.ds(1, FBC)]
    rim_below = p_v.at[FBR + 1, pl.ds(1, FBC)]

    def rim_column(at):
        return p_v.at[pl.ds(1, FBR), at]

    up = halo(0, p_hbm.at[0], rim_below, (row - 1, col))
    down = halo(1, p_hbm.at[FBR - 1], rim_above, (row + 1, col))
    across = halo(2, p_hbm.at[:, (FBC - 1) * odd], rim_column((FBC + 1) * (1 - odd)), (row, far))
    beside = halo(3, p_hbm.at[:, (FBC - 1) * (1 - odd)], rim_column((FBC + 1) * odd), (row, near))
    up_in = halo(0, p_hbm.at[0], rim_below, (row - 1, col))
    down_in = halo(1, p_hbm.at[0], rim_above, (row + 1, col))
    across_in = halo(2, p_hbm.at[:, 0], rim_column((FBC + 1) * odd), (row, far))
    beside_in = halo(3, p_hbm.at[:, 0], rim_column((FBC + 1) * (1 - odd)), (row, near))

    count = 1 + has_above.astype(jnp.int32) + has_below.astype(jnp.int32) + has_far.astype(jnp.int32)
    pl.semaphore_wait(barrier, count)
    pl.when(has_above)(up.start)
    pl.when(has_below)(down.start)
    pl.when(has_far)(across.start)
    beside.start()

    @pl.when(jnp.logical_not(has_above))
    def _():
        rim_above[...] = jnp.zeros(rim_above.shape, BF16)

    @pl.when(jnp.logical_not(has_below))
    def _():
        rim_below[...] = jnp.zeros(rim_below.shape, BF16)

    @pl.when(jnp.logical_not(has_far))
    def _():
        edge = (FBC + 1) * odd
        for r in range(FBR):
            p_v[1 + r, edge] = jnp.zeros((KP, B, B), BF16)

    load_slot.wait()
    load_p.wait()

    def transpose_half(half, carry):
        for i in range(2):
            r = (1 - half) * (1 + i) + half * 3 * i
            for c in range(FBC):
                for p in range(KP):
                    turned = p_v[1 + r, 1 + c, p].T
                    label = slot[r, c, p, p, SELF] - col * CTD
                    at = ((i * FBC + c) * KP + p) * B
                    for o, shift in enumerate((to_far, to_near, 0)):
                        for aggregate in range(2):
                            keep = jnp.where(label == shift * CTD + 3 * aggregate, 1.0, 0.0)
                            pt[o, half, aggregate * B : (aggregate + 1) * B, at : at + B] = turned * keep.astype(BF16)
        return carry

    lax.fori_loop(0, 2, transpose_half, 0)

    def products(r, c, k, rim_r, rim_c):
        right = jnp.concatenate([p_v[rim_r, rim_c, 0], p_v[rim_r, rim_c, 1]], axis=1)
        ap = jnp.dot(a_v[r, c, k], right, preferred_element_type=F32).astype(BF16).astype(F32)
        tiles = [ap[:, :B], ap[:, B:]]
        sums = [tiles[0] + tiles[1]]
        for p in range(KP):
            base = slot[r, c, p, p, SELF]
            for kind in range(2):
                keep = [jnp.where(slot[r, c, p, q, k] == base + kind, 1.0, 0.0) for q in range(KP)]
                sums.append(tiles[0] * keep[0] + tiles[1] * keep[1])
        return sums

    def add(one, other):
        return [x + y for x, y in zip(one, other)]

    def held(r, c):
        return [acc[r, c, n] for n in range(5)]

    def hold(r, c, sums):
        for n in range(5):
            acc[r, c, n] = sums[n]

    def finish(r, c, sums):
        half, i = place(r)
        for p in range(KP):
            first, second = sums[1 + 2 * p], sums[2 + 2 * p]
            at = ((i * FBC + c) * KP + p) * B
            g[half, at : at + B, :B] = first.astype(BF16)
            g[half, at : at + B, B : 2 * B] = second.astype(BF16)
            g[half, at : at + B, 2 * B :] = (sums[0] - first - second).astype(BF16)

    load_a.wait()

    def within_row(r, carry):
        for c in range(FBC):
            sums = products(r, c, SELF, r + 1, c + 1)
            if c > 0:
                sums = add(sums, products(r, c, LEFT, r + 1, c))
            if c < FBC - 1:
                sums = add(sums, products(r, c, RIGHT, r + 1, c + 2))
            hold(r, c, sums)
        return carry

    lax.fori_loop(0, FBR, within_row, 0)

    def between_rows(r, carry):
        for c in range(FBC):
            hold(r, c, add(held(r, c), products(r, c, BELOW, r + 2, c + 1)))
            hold(r + 1, c, add(held(r + 1, c), products(r + 1, c, ABOVE, r + 1, c + 1)))
        return carry

    lax.fori_loop(0, FBR - 1, between_rows, 0)

    beside_in.wait_recv()
    pl.when(has_far)(across_in.wait_recv)

    for r in range(FBR):
        left = add(held(r, 0), products(r, 0, LEFT, r + 1, 0))
        right = add(held(r, FBC - 1), products(r, FBC - 1, RIGHT, r + 1, FBC + 1))
        if r in (1, 2):
            finish(r, 0, left)
            finish(r, 1, held(r, 1))
            finish(r, 2, right)
        else:
            hold(r, 0, left)
            hold(r, FBC - 1, right)

    def first_half(o, carry):
        part[o] = jnp.dot(pt[o, 0], g[0], preferred_element_type=F32)
        return carry

    lax.fori_loop(0, 3, first_half, 0)

    pl.when(has_above)(down_in.wait_recv)
    pl.when(has_below)(up_in.wait_recv)
    for c in range(FBC):
        finish(0, c, add(held(0, c), products(0, c, ABOVE, 0, c + 1)))
        finish(FBR - 1, c, add(held(FBR - 1, c), products(FBR - 1, c, BELOW, FBR + 1, c + 1)))

    def partial_tiles(o, target):
        total = part[o] + jnp.dot(pt[o, 1], g[1], preferred_element_type=F32)
        for aggregate in range(2):
            for kind in range(3):
                tile = total[aggregate * B : (aggregate + 1) * B, kind * B : (kind + 1) * B]
                target[3 * aggregate + kind] = tile.astype(target.dtype)

    def partial(index, target, there):
        return pltpu.make_async_remote_copy(
            src_ref=out_v.at[index], dst_ref=target, send_sem=part_send.at[index], recv_sem=part_recv.at[index],
            device_id=there, device_id_type=MESH)

    to_far_copy = partial(0, far_hbm, (row, far))
    to_near_copy = partial(1, near_hbm, (row, near))
    partial_tiles(0, out_v.at[0])
    pl.when(has_far)(to_far_copy.start)

    @pl.when(jnp.logical_not(has_far))
    def _():
        out_v[0] = jnp.zeros((CTD, B, B), BF16)
        fill = pltpu.make_async_copy(out_v.at[0], far_hbm, store_sem.at[1])
        fill.start()
        fill.wait()

    partial_tiles(1, out_v.at[1])
    to_near_copy.start()
    partial_tiles(2, mine_v)
    store = pltpu.make_async_copy(mine_v, mine_hbm, store_sem.at[0])
    store.start()

    pl.when(has_above)(up.wait_send)
    pl.when(has_below)(down.wait_send)
    pl.when(has_far)(across.wait_send)
    beside.wait_send()
    to_near_copy.wait()
    store.wait()
    pl.when(has_far)(to_far_copy.wait)


def body(n_row, n_col, a_tiles, p_tiles, c_slot):
    any_space, hbm = pl.BlockSpec(memory_space=pl.ANY), pl.BlockSpec(memory_space=pltpu.HBM)
    mine, far, near = pl.pallas_call(
        functools.partial(kernel, n_row, n_col),
        out_shape=[
            jax.ShapeDtypeStruct((CTD, B, B), F32),
            jax.ShapeDtypeStruct((CTD, B, B), BF16),
            jax.ShapeDtypeStruct((CTD, B, B), BF16),
        ],
        in_specs=[hbm, hbm, hbm],
        out_specs=[any_space] * 3,
        scratch_shapes=[
            pltpu.SMEM((FBR, FBC, KP, KP, 5), jnp.int32),
            pltpu.VMEM((FBR, FBC, 5, B, B), BF16),
            pltpu.VMEM((FBR + 2, FBC + 2, KP, B, B), BF16),
            pltpu.VMEM((FBR, FBC, 5, B, B), F32),
            pltpu.VMEM((3, 2, 2 * B, 2 * FBC * KP * B), BF16),
            pltpu.VMEM((2, 2 * FBC * KP * B, 3 * B), BF16),
            pltpu.VMEM((3, 2 * B, 3 * B), F32),
            pltpu.VMEM((CTD, B, B), F32),
            pltpu.VMEM((2, CTD, B, B), BF16),
            pltpu.SemaphoreType.DMA((3,)),
            pltpu.SemaphoreType.DMA((4,)),
            pltpu.SemaphoreType.DMA((4,)),
            pltpu.SemaphoreType.DMA((2,)),
            pltpu.SemaphoreType.DMA((2,)),
            pltpu.SemaphoreType.DMA((2,)),
        ],
        compiler_params=pltpu.CompilerParams(
            collective_id=0, has_side_effects=True, vmem_limit_bytes=48 * 1024 * 1024),
        name="coarse",
    )(a_tiles, p_tiles, jnp.swapaxes(c_slot, 3, 4))
    return mine + far.astype(F32) + near.astype(F32)


def solution(mesh):
    spec = P("row", "col", None, None, None)
    return jax.shard_map(
        functools.partial(body, mesh.shape["row"], mesh.shape["col"]), mesh=mesh, in_specs=(spec, spec, spec),
        out_specs=P(("row", "col"), None, None), check_vma=False)
```

time: 100 us -> 32.1 us (0.32)
  the two profiles are of different devices: /device:TPU:447 before, /device:TPU:1 now
where the time goes in v1:
time: 32.1 us; the launch traced here: 31.8 us
  Pallas kernels  27.6 us (86%)
  local copies, waits for them, and re-layouts  3.41 us (11%)
  other arithmetic  0.8 us (2%)
    pallas_call x1, Pallas kernels, body(): pl.pallas_call(functools.partial(kernel, n_row, n_col), out_shape=[jax.Sh...  27.6 us
    unnamed x6, local copies, waits for them, and re-layouts  3.41 us
    add x1, other arithmetic, body(): return mine + far.astype(F32) + near.astype(F32)  0.8 us

profile of v1, /device:TPU:1, one launch (start us, length us, event | category | flops | bytes accessed | tf_op | source)
XLA Modules:
  0.0 31.8 jit_solution(4029424846140482221)
XLA Ops:
  0.0 0.0 copy-start
  0.0 1.5 %copy-done = bf16[4,3,5,128,128]{4,3,2,1,0:T(8,128)(2,1)S(1)} copy-done((bf16[4,3,5,128,128]{4,3,2,1,0:T(8,128)(2,1)S(1)}, bf16[4,3,5,128,128]{4,3,2,1,0:T(8,128)(2,1)}, u32[]{:S(2)}) %copy-start) | copy-done | bytes 1966104
  1.5 0.0 copy-start.1
  1.5 1.1 %copy-done.1 = bf16[4,3,2,128,128]{4,3,2,1,0:T(8,128)(2,1)S(1)} copy-done((bf16[4,3,2,128,128]{4,3,2,1,0:T(8,128)(2,1)S(1)}, bf16[4,3,2,128,128]{4,3,2,1,0:T(8,128)(2,1)}, u32[]{:S(2)}) %copy-start.1) | copy-done | bytes 786456
  2.7 0.0 copy-start.2
  2.7 0.7 %copy-done.2 = s32[4,3,2,5,2]{3,4,2,1,0:T(2,128)S(1)} copy-done((s32[4,3,2,5,2]{3,4,2,1,0:T(2,128)S(1)}, s32[4,3,2,5,2]{3,4,2,1,0:T(2,128)}, u32[]{:S(2)}) %copy-start.2) | copy-done | bytes 984
  3.4 27.6 %coarse.1 = (f32[6,128,128]{2,1,0:T(8,128)S(1)}, bf16[6,128,128]{2,1,0:T(8,128)(2,1)S(1)}, bf16[6,128,128]{2,1,0:T(8,128)(2,1)S(1)}) custom-call(bf16[4,3,5,128,128]{4,3,2,1,0:T(8,128)(2,1)S(1)} %copy-done, bf16[4,3,2,128,128]{4,3,2,1,0:T(8,128)(2,1)S(1)} %copy-done.1, s32[4,3,2,2,5]{4,3,2,1,0:T(2,128)S(1)} %bitcast.1), custom_call_target="tpu_custom_call" | custom-call | tf_op jit(solution)/shard_map/coarse/pallas_call | solution.py:230
  31.0 0.8 %convert_add_fusion = f32[6,128,128]{2,1,0:T(8,128)} fusion(bf16[6,128,128]{2,1,0:T(8,128)(2,1)S(1)} %get-tuple-element.10, f32[6,128,128]{2,1,0:T(8,128)S(1)} %get-tuple-element.8, bf16[6,128,128]{2,1,0:T(8,128)(2,1)S(1)} %get-tuple-element.9), kind=kLoop, calls=%fused_computation | loop fusion | flops 393216 | bytes 1179648 | tf_op jit(solution)/shard_map/add | solution.py:260
Async XLA Ops:
  0.0 1.5 %copy-start = (bf16[4,3,5,128,128]{4,3,2,1,0:T(8,128)(2,1)S(1)}, bf16[4,3,5,128,128]{4,3,2,1,0:T(8,128)(2,1)}, u32[]{:S(2)}) copy-start(bf16[4,3,5,128,128]{4,3,2,1,0:T(8,128)(2,1)} %a_hbm.1) | copy-start | bytes 5898244
  1.5 1.1 %copy-start.1 = (bf16[4,3,2,128,128]{4,3,2,1,0:T(8,128)(2,1)S(1)}, bf16[4,3,2,128,128]{4,3,2,1,0:T(8,128)(2,1)}, u32[]{:S(2)}) copy-start(bf16[4,3,2,128,128]{4,3,2,1,0:T(8,128)(2,1)} %p_hbm.1) | copy-start | bytes 2359300
  2.7 0.7 %copy-start.2 = (s32[4,3,2,5,2]{3,4,2,1,0:T(2,128)S(1)}, s32[4,3,2,5,2]{3,4,2,1,0:T(2,128)}, u32[]{:S(2)}) copy-start(s32[4,3,2,5,2]{3,4,2,1,0:T(2,128)} %param.5) | copy-start | bytes 2884

commit v2 on v1

v2 whole, which is shorter than its diff:
```python
import functools

import jax
import jax.numpy as jnp
from jax import lax
from jax.experimental import pallas as pl
from jax.experimental.pallas import tpu as pltpu
from jax.sharding import PartitionSpec as P

MESH = pl.DeviceIdType.MESH
B = 128
KP = 2
FBR = 4
FBC = 3
CTD = 6
SELF, ABOVE, BELOW, LEFT, RIGHT = range(5)
F32, BF16 = jnp.float32, jnp.bfloat16


def kernel(n_row, n_col, a_hbm, p_hbm, slot_hbm, mine, far_hbm, near_hbm, slot, a_v, p_v, acc, pt, chain, out_v,
           load_sem, halo_send, halo_recv, part_send, part_recv, fill_sem):
    row, col = lax.axis_index("row"), lax.axis_index("col")
    odd = lax.rem(col, 2)
    far, near = col - 1 + 2 * odd, col + 1 - 2 * odd
    has_above, has_below = row > 0, row < n_row - 1
    has_far = jnp.logical_and(far >= 0, far < n_col)

    barrier = pltpu.get_barrier_semaphore()

    def greet(there):
        pl.semaphore_signal(barrier, inc=1, device_id=there, device_id_type=MESH)

    pl.when(has_above)(lambda: greet((row - 1, col)))
    pl.when(has_below)(lambda: greet((row + 1, col)))
    pl.when(has_far)(lambda: greet((row, far)))

    load_slot = pltpu.make_async_copy(slot_hbm, slot, load_sem.at[2 * FBR])
    load_slot.start()

    def load_p(r):
        return pltpu.make_async_copy(p_hbm.at[r], p_v.at[1 + r, pl.ds(1, FBC)], load_sem.at[FBR + r])

    def load_a(r):
        return pltpu.make_async_copy(a_hbm.at[r], a_v.at[r], load_sem.at[r])

    for r in range(FBR):
        load_p(r).start()
    for r in range(FBR):
        load_a(r).start()

    def halo(index, source, target, there):
        return pltpu.make_async_remote_copy(
            src_ref=source, dst_ref=target, send_sem=halo_send.at[index], recv_sem=halo_recv.at[index],
            device_id=there, device_id_type=MESH)

    rim_above = p_v.at[0, pl.ds(1, FBC)]
    rim_below = p_v.at[FBR + 1, pl.ds(1, FBC)]

    def rim_column(at):
        return p_v.at[pl.ds(1, FBR), at]

    up = halo(0, p_hbm.at[0], rim_below, (row - 1, col))
    down = halo(1, p_hbm.at[FBR - 1], rim_above, (row + 1, col))
    across = halo(2, p_hbm.at[:, (FBC - 1) * odd], rim_column((FBC + 1) * (1 - odd)), (row, far))
    beside = halo(3, p_hbm.at[:, (FBC - 1) * (1 - odd)], rim_column((FBC + 1) * odd), (row, near))
    up_in = halo(0, p_hbm.at[0], rim_below, (row - 1, col))
    down_in = halo(1, p_hbm.at[0], rim_above, (row + 1, col))
    across_in = halo(2, p_hbm.at[:, 0], rim_column((FBC + 1) * odd), (row, far))
    beside_in = halo(3, p_hbm.at[:, 0], rim_column((FBC + 1) * (1 - odd)), (row, near))

    count = 1 - odd + has_above.astype(jnp.int32) + has_below.astype(jnp.int32) + has_far.astype(jnp.int32)
    pl.semaphore_wait(barrier, count)
    greet((row, near))
    pl.when(has_far)(across.start)
    pl.when(has_above)(up.start)
    pl.when(has_below)(down.start)
    pl.when(odd == 0)(beside.start)

    @pl.when(jnp.logical_not(has_above))
    def _():
        rim_above[...] = jnp.zeros(rim_above.shape, BF16)

    @pl.when(jnp.logical_not(has_below))
    def _():
        rim_below[...] = jnp.zeros(rim_below.shape, BF16)

    fill = pltpu.make_async_copy(out_v.at[1], far_hbm, fill_sem)

    @pl.when(jnp.logical_not(has_far))
    def _():
        edge = (FBC + 1) * odd
        for r in range(FBR):
            p_v[1 + r, edge] = jnp.zeros((KP, B, B), BF16)
        out_v[1] = jnp.zeros((CTD, B, B), BF16)
        fill.start()

    chain[0] = jnp.zeros((B, 3 * B), F32)
    def transpose_row(r, carry):
        load_p(r).wait()
        for c in range(FBC):
            for p in range(KP):
                pt[r, c, p] = p_v[1 + r, 1 + c, p].T
        return carry

    lax.fori_loop(0, FBR, transpose_row, 0)
    load_slot.wait()

    def products(r, c, k, rim_r, rim_c):
        right = jnp.concatenate([p_v[rim_r, rim_c, 0], p_v[rim_r, rim_c, 1]], axis=1)
        ap = jnp.dot(a_v[r, c, k], right, preferred_element_type=F32).astype(BF16).astype(F32)
        tiles = [ap[:, :B], ap[:, B:]]
        sums = [tiles[0] + tiles[1]]
        for p in range(KP):
            base = slot[r, c, p, p, SELF]
            for kind in range(2):
                keep = [jnp.where(slot[r, c, p, q, k] == base + kind, 1.0, 0.0) for q in range(KP)]
                sums.append(tiles[0] * keep[0] + tiles[1] * keep[1])
        return sums

    def add(one, other):
        return [x + y for x, y in zip(one, other)]

    def held(r, c):
        return [acc[r, c, n] for n in range(5)]

    def hold(r, c, sums):
        for n in range(5):
            acc[r, c, n] = sums[n]

    def gather(r, c, sums, last):
        for p in range(KP):
            first, second = sums[1 + 2 * p], sums[2 + 2 * p]
            kinds = jnp.concatenate([first, second, sums[0] - first - second], axis=1).astype(BF16)
            term = jnp.dot(pt[r, c, p], kinds, preferred_element_type=F32)
            label = slot[r, c, p, p, SELF] - (col - 1) * CTD
            at = 1 + (r * FBC + c) * KP + p
            before = jnp.int32(0)
            for n in range(6):
                before = jnp.where(label == 3 * n, last[n], before)
            last = [jnp.where(label == 3 * n, at, last[n]) for n in range(6)]
            chain[at] = term + chain[before]
        return last

    def within_row(r, carry):
        load_a(r).wait()
        for c in range(FBC):
            sums = products(r, c, SELF, r + 1, c + 1)
            if c > 0:
                sums = add(sums, products(r, c, LEFT, r + 1, c))
            if c < FBC - 1:
                sums = add(sums, products(r, c, RIGHT, r + 1, c + 2))
            hold(r, c, sums)
        return carry

    lax.fori_loop(0, FBR, within_row, 0)

    def between_rows(r, carry):
        for c in range(FBC):
            hold(r, c, add(held(r, c), products(r, c, BELOW, r + 2, c + 1)))
            hold(r + 1, c, add(held(r + 1, c), products(r + 1, c, ABOVE, r + 1, c + 1)))
        return carry

    lax.fori_loop(0, FBR - 1, between_rows, 0)

    @pl.when(odd == 1)
    def _():
        pl.semaphore_wait(barrier, 1)
        beside.start()

    beside_in.wait_recv()
    pl.when(has_far)(across_in.wait_recv)

    def along_row(r):
        left = add(held(r, 0), products(r, 0, LEFT, r + 1, 0))
        right = add(held(r, FBC - 1), products(r, FBC - 1, RIGHT, r + 1, FBC + 1))
        return left, right

    last = [jnp.int32(0)] * 6

    def inner_row(r, last):
        left, right = along_row(r)
        for c, sums in enumerate((left, held(r, 1), right)):
            last = gather(r, c, sums, last)
        return last

    last = lax.fori_loop(1, FBR - 1, inner_row, last)
    for r in (0, FBR - 1):
        left, right = along_row(r)
        hold(r, 0, left)
        hold(r, FBC - 1, right)

    pl.when(has_above)(down_in.wait_recv)
    pl.when(has_below)(up_in.wait_recv)
    for r, k, rim in ((0, ABOVE, 0), (FBR - 1, BELOW, FBR + 1)):
        for c in range(FBC):
            last = gather(r, c, add(held(r, c), products(r, c, k, rim, c + 1)), last)

    def partial_tiles(owner, target):
        for aggregate in range(2):
            total = chain[jnp.where(owner == -1, last[aggregate], jnp.where(owner == 0, last[2 + aggregate], last[4 + aggregate]))]
            for kind in range(3):
                target[3 * aggregate + kind] = total[:, kind * B : (kind + 1) * B].astype(target.dtype)

    def partial(index, target, there):
        return pltpu.make_async_remote_copy(
            src_ref=out_v.at[index], dst_ref=target, send_sem=part_send.at[index], recv_sem=part_recv.at[index],
            device_id=there, device_id_type=MESH)

    to_near_copy = partial(0, near_hbm, (row, near))
    to_far_copy = partial(1, far_hbm, (row, far))
    partial_tiles(near - col, out_v.at[0])
    to_near_copy.start()

    @pl.when(has_far)
    def _():
        partial_tiles(far - col, out_v.at[1])
        to_far_copy.start()

    partial_tiles(0, mine)

    pl.when(has_above)(up.wait_send)
    pl.when(has_below)(down.wait_send)
    pl.when(has_far)(across.wait_send)
    beside.wait_send()
    pl.when(jnp.logical_not(has_far))(fill.wait)
    to_near_copy.wait()
    pl.when(has_far)(to_far_copy.wait)


def body(n_row, n_col, a_tiles, p_tiles, c_slot):
    any_space, hbm = pl.BlockSpec(memory_space=pl.ANY), pl.BlockSpec(memory_space=pltpu.HBM)
    operands = [
        pltpu.with_memory_space_constraint(x, pltpu.HBM) for x in (a_tiles, p_tiles, jnp.swapaxes(c_slot, 3, 4))
    ]
    mine, far, near = pl.pallas_call(
        functools.partial(kernel, n_row, n_col),
        out_shape=[
            jax.ShapeDtypeStruct((CTD, B, B), F32),
            jax.ShapeDtypeStruct((CTD, B, B), BF16),
            jax.ShapeDtypeStruct((CTD, B, B), BF16),
        ],
        in_specs=[hbm, hbm, hbm],
        out_specs=[pl.BlockSpec(memory_space=pltpu.VMEM), any_space, any_space],
        scratch_shapes=[
            pltpu.SMEM((FBR, FBC, KP, KP, 5), jnp.int32),
            pltpu.VMEM((FBR, FBC, 5, B, B), BF16),
            pltpu.VMEM((FBR + 2, FBC + 2, KP, B, B), BF16),
            pltpu.VMEM((FBR, FBC, 5, B, B), F32),
            pltpu.VMEM((FBR, FBC, KP, B, B), BF16),
            pltpu.VMEM((1 + FBR * FBC * KP, B, 3 * B), F32),
            pltpu.VMEM((2, CTD, B, B), BF16),
            pltpu.SemaphoreType.DMA((2 * FBR + 1,)),
            pltpu.SemaphoreType.DMA((4,)),
            pltpu.SemaphoreType.DMA((4,)),
            pltpu.SemaphoreType.DMA((2,)),
            pltpu.SemaphoreType.DMA((2,)),
            pltpu.SemaphoreType.DMA,
        ],
        compiler_params=pltpu.CompilerParams(
            collective_id=0, has_side_effects=True, vmem_limit_bytes=48 * 1024 * 1024),
        name="coarse",
    )(*operands)
    return mine + far.astype(F32) + near.astype(F32)


def solution(mesh):
    spec = P("row", "col", None, None, None)
    return jax.shard_map(
        functools.partial(body, mesh.shape["row"], mesh.shape["col"]), mesh=mesh, in_specs=(spec, spec, spec),
        out_specs=P(("row", "col"), None, None), check_vma=False)
```

time: 32.1 us -> 24.4 us (0.76)
  Pallas kernels: 27.6 us -> 23.4 us
  local copies, waits for them, and re-layouts: 3.41 us -> 0 us
    pallas_call x1, Pallas kernels: 27.6 us -> 23.4 us  [body(): pl.pallas_call(functools.partial(kernel, n_row, n_col), out_shape=[jax.Sh...]
    unnamed x6 -> x0, local copies, waits for them, and re-layouts: 3.41 us -> none
where the time goes in v2:
time: 24.4 us; the launch traced here: 24.2 us
  Pallas kernels  23.4 us (96%)
  other arithmetic  0.8 us (3%)
    pallas_call x1, Pallas kernels, body(): pl.pallas_call(functools.partial(kernel, n_row, n_col), out_shape=[jax.Sh...  23.4 us
    add x1, other arithmetic, body(): return mine + far.astype(F32) + near.astype(F32)  0.8 us

profile of v2, /device:TPU:1, one launch (start us, length us, event | category | flops | bytes accessed | tf_op | source)
XLA Modules:
  0.0 24.2 jit_solution(4014875626064913830)
XLA Ops:
  0.0 23.4 %coarse.1 = (f32[6,128,128]{2,1,0:T(8,128)S(1)}, bf16[6,128,128]{2,1,0:T(8,128)(2,1)S(1)}, bf16[6,128,128]{2,1,0:T(8,128)(2,1)S(1)}) custom-call(bf16[4,3,5,128,128]{4,3,2,1,0:T(8,128)(2,1)} %a_hbm.1, bf16[4,3,2,128,128]{4,3,2,1,0:T(8,128)(2,1)} %p_hbm.1, s32[4,3,2,2,5]{4,3,2,1,0:T(2,128)} %bitcast.1), custom_call_target="tpu_custom_call" | custom-call | tf_op jit(solution)/shard_map/coarse/pallas_call | solution.py:235
  23.4 0.8 %convert_add_fusion = f32[6,128,128]{2,1,0:T(8,128)} fusion(bf16[6,128,128]{2,1,0:T(8,128)(2,1)S(1)} %get-tuple-element.10, f32[6,128,128]{2,1,0:T(8,128)S(1)} %get-tuple-element.8, bf16[6,128,128]{2,1,0:T(8,128)(2,1)S(1)} %get-tuple-element.9), kind=kLoop, calls=%fused_computation | loop fusion | flops 393216 | bytes 1179648 | tf_op jit(solution)/shard_map/add | solution.py:263

commit v3 on v2

--- a/solution.py
+++ b/solution.py
@@ -45,7 +45,7 @@
 
     for r in range(FBR):
         load_p(r).start()
-    for r in range(FBR):
+    for r in (1, 2, 0, 3):
         load_a(r).start()
 
     def halo(index, source, target, there):
@@ -68,13 +68,16 @@
     across_in = halo(2, p_hbm.at[:, 0], rim_column((FBC + 1) * odd), (row, far))
     beside_in = halo(3, p_hbm.at[:, 0], rim_column((FBC + 1) * (1 - odd)), (row, near))
 
-    count = 1 - odd + has_above.astype(jnp.int32) + has_below.astype(jnp.int32) + has_far.astype(jnp.int32)
-    pl.semaphore_wait(barrier, count)
-    greet((row, near))
-    pl.when(has_far)(across.start)
-    pl.when(has_above)(up.start)
-    pl.when(has_below)(down.start)
-    pl.when(odd == 0)(beside.start)
+    def meet():
+        count = 1 - odd + has_above.astype(jnp.int32) + has_below.astype(jnp.int32) + has_far.astype(jnp.int32)
+        pl.semaphore_wait(barrier, count)
+        greet((row, near))
+        pl.when(has_far)(across.start)
+        pl.when(has_above)(up.start)
+        pl.when(has_below)(down.start)
+        pl.when(odd == 0)(beside.start)
+
+    pl.when(row != 1)(meet)
 
     @pl.when(jnp.logical_not(has_above))
     def _():
@@ -113,6 +116,10 @@
         for p in range(KP):
             base = slot[r, c, p, p, SELF]
             for kind in range(2):
+                if k is SELF:
+                    other = tiles[1 - p] * jnp.where(slot[r, c, p, 1 - p, k] == base + kind, 1.0, 0.0)
+                    sums.append(tiles[p] + other if kind == 0 else other)
+                    continue
                 keep = [jnp.where(slot[r, c, p, q, k] == base + kind, 1.0, 0.0) for q in range(KP)]
                 sums.append(tiles[0] * keep[0] + tiles[1] * keep[1])
         return sums
@@ -141,7 +148,7 @@
             chain[at] = term + chain[before]
         return last
 
-    def within_row(r, carry):
+    def interior(r, verticals):
         load_a(r).wait()
         for c in range(FBC):
             sums = products(r, c, SELF, r + 1, c + 1)
@@ -149,51 +156,81 @@
                 sums = add(sums, products(r, c, LEFT, r + 1, c))
             if c < FBC - 1:
                 sums = add(sums, products(r, c, RIGHT, r + 1, c + 2))
+            for k, rim in verticals:
+                sums = add(sums, products(r, c, k, rim, c + 1))
             hold(r, c, sums)
+
+    def inner_interior(r, carry):
+        interior(r, ((ABOVE, r), (BELOW, r + 2)))
         return carry
 
-    lax.fori_loop(0, FBR, within_row, 0)
-
-    def between_rows(r, carry):
-        for c in range(FBC):
-            hold(r, c, add(held(r, c), products(r, c, BELOW, r + 2, c + 1)))
-            hold(r + 1, c, add(held(r + 1, c), products(r + 1, c, ABOVE, r + 1, c + 1)))
+    def outer_interior(i, carry):
+        interior((FBR - 1) * i, ((BELOW - i, 2 + i),))
         return carry
 
-    lax.fori_loop(0, FBR - 1, between_rows, 0)
-
-    @pl.when(odd == 1)
-    def _():
+    lax.fori_loop(1, FBR - 1, inner_interior, 0)
+    pl.when(row == 1)(meet)
+    lax.fori_loop(0, 2, outer_interior, 0)
+
+    first, final = 0, FBR - 1
+    inner = range(1, FBR - 1)
+
+    def with_side(r, c):
+        k, rim = (LEFT, 0) if c == 0 else (RIGHT, FBC + 1)
+        return add(held(r, c), products(r, c, k, r + 1, rim))
+
+    def with_end(r, c):
+        k, rim = (ABOVE, 0) if r == first else (BELOW, FBR + 1)
+        return add(held(r, c), products(r, c, k, rim, c + 1))
+
+    def hold_all(sums_of, blocks):
+        for r, c in blocks:
+            hold(r, c, sums_of(r, c))
+
+    def gather_all(sums_of, blocks, last):
+        for r, c in blocks:
+            last = gather(r, c, sums_of(r, c), last)
+        return last
+
+    def column(c, rows=range(FBR)):
+        return [(r, c) for r in rows]
+
+    def far_side(c):
+        @pl.when(has_far)
+        def _():
+            across_in.wait_recv()
+            hold_all(with_side, column(c))
+
+    def even_order(last):
+        far_side(0)
+        last = gather_all(held, column(0, inner) + column(1, inner), last)
+        beside_in.wait_recv()
+        hold_all(with_side, column(2, (first, final)))
+        last = gather_all(with_side, column(2, inner), last)
+
+        @pl.when(has_above)
+        def _():
+            down_in.wait_recv()
+            hold_all(with_end, [(first, c) for c in range(FBC)])
+
+        last = gather_all(held, [(first, c) for c in range(FBC)], last)
+        pl.when(has_below)(up_in.wait_recv)
+        return gather_all(with_end, [(final, c) for c in range(FBC)], last)
+
+    def odd_order(last):
+        far_side(2)
+        last = gather_all(held, column(1, inner) + column(2, inner), last)
         pl.semaphore_wait(barrier, 1)
         beside.start()
-
-    beside_in.wait_recv()
-    pl.when(has_far)(across_in.wait_recv)
-
-    def along_row(r):
-        left = add(held(r, 0), products(r, 0, LEFT, r + 1, 0))
-        right = add(held(r, FBC - 1), products(r, FBC - 1, RIGHT, r + 1, FBC + 1))
-        return left, right
-
-    last = [jnp.int32(0)] * 6
-
-    def inner_row(r, last):
-        left, right = along_row(r)
-        for c, sums in enumerate((left, held(r, 1), right)):
-            last = gather(r, c, sums, last)
-        return last
-
-    last = lax.fori_loop(1, FBR - 1, inner_row, last)
-    for r in (0, FBR - 1):
-        left, right = along_row(r)
-        hold(r, 0, left)
-        hold(r, FBC - 1, right)
-
-    pl.when(has_above)(down_in.wait_recv)
-    pl.when(has_below)(up_in.wait_recv)
-    for r, k, rim in ((0, ABOVE, 0), (FBR - 1, BELOW, FBR + 1)):
-        for c in range(FBC):
-            last = gather(r, c, add(held(r, c), products(r, c, k, rim, c + 1)), last)
+        pl.when(has_above)(down_in.wait_recv)
+        pl.when(has_below)(up_in.wait_recv)
+        hold_all(with_end, [(first, 0), (final, 0)])
+        last = gather_all(with_end, [(r, c) for c in (1, 2) for r in (first, final)], last)
+
+        beside_in.wait_recv()
+        return gather_all(with_side, column(0), last)
+
+    last = lax.cond(odd == 1, odd_order, even_order, [jnp.int32(0)] * 6)
 
     def partial_tiles(owner, target):
         for aggregate in range(2):

time: 24.4 us -> 23.7 us (0.971)
  Pallas kernels: 23.4 us -> 22.8 us
    pallas_call x1, Pallas kernels: 23.4 us -> 22.8 us  [body(): pl.pallas_call(functools.partial(kernel, n_row, n_col), out_shape=[jax.Sh...]
where the time goes in v3:
time: 23.7 us; the launch traced here: 23.6 us
  Pallas kernels  22.8 us (96%)
  other arithmetic  0.8 us (3%)
    pallas_call x1, Pallas kernels, body(): pl.pallas_call(functools.partial(kernel, n_row, n_col), out_shape=[jax.Sh...  22.8 us
    add x1, other arithmetic, body(): return mine + far.astype(F32) + near.astype(F32)  0.8 us

profile of v3, /device:TPU:1, one launch (start us, length us, event | category | flops | bytes accessed | tf_op | source)
XLA Modules:
  0.0 23.6 jit_solution(3593510827962814983)
XLA Ops:
  0.0 22.8 %coarse.1 = (f32[6,128,128]{2,1,0:T(8,128)S(1)}, bf16[6,128,128]{2,1,0:T(8,128)(2,1)S(1)}, bf16[6,128,128]{2,1,0:T(8,128)(2,1)S(1)}) custom-call(bf16[4,3,5,128,128]{4,3,2,1,0:T(8,128)(2,1)} %a_hbm.1, bf16[4,3,2,128,128]{4,3,2,1,0:T(8,128)(2,1)} %p_hbm.1, s32[4,3,2,2,5]{4,3,2,1,0:T(2,128)} %bitcast.1), custom_call_target="tpu_custom_call" | custom-call | tf_op jit(solution)/shard_map/coarse/pallas_call | solution.py:272
  22.8 0.8 %convert_add_fusion = f32[6,128,128]{2,1,0:T(8,128)} fusion(bf16[6,128,128]{2,1,0:T(8,128)(2,1)S(1)} %get-tuple-element.10, f32[6,128,128]{2,1,0:T(8,128)S(1)} %get-tuple-element.8, bf16[6,128,128]{2,1,0:T(8,128)(2,1)S(1)} %get-tuple-element.9), kind=kLoop, calls=%fused_computation | loop fusion | flops 393216 | bytes 1179648 | tf_op jit(solution)/shard_map/add | solution.py:300

commit v4 on v3

--- a/solution.py
+++ b/solution.py
@@ -17,7 +17,7 @@
 F32, BF16 = jnp.float32, jnp.bfloat16
 
 
-def kernel(n_row, n_col, a_hbm, p_hbm, slot_hbm, mine, far_hbm, near_hbm, slot, a_v, p_v, acc, pt, chain, out_v,
+def kernel(n_row, n_col, a_hbm, p_hbm, slot_hbm, mine, far_hbm, near_hbm, slot, before, a_v, p_v, acc, pt, chain, out_v,
            load_sem, halo_send, halo_recv, part_send, part_recv, fill_sem):
     row, col = lax.axis_index("row"), lax.axis_index("col")
     odd = lax.rem(col, 2)
@@ -59,25 +59,33 @@
     def rim_column(at):
         return p_v.at[pl.ds(1, FBR), at]
 
-    up = halo(0, p_hbm.at[0], rim_below, (row - 1, col))
-    down = halo(1, p_hbm.at[FBR - 1], rim_above, (row + 1, col))
-    across = halo(2, p_hbm.at[:, (FBC - 1) * odd], rim_column((FBC + 1) * (1 - odd)), (row, far))
-    beside = halo(3, p_hbm.at[:, (FBC - 1) * (1 - odd)], rim_column((FBC + 1) * odd), (row, near))
+    def outgoing(row_at, column_at):
+        return (
+            halo(0, row_at(0), rim_below, (row - 1, col)),
+            halo(1, row_at(FBR - 1), rim_above, (row + 1, col)),
+            halo(2, column_at((FBC - 1) * odd), rim_column((FBC + 1) * (1 - odd)), (row, far)),
+            halo(3, column_at((FBC - 1) * (1 - odd)), rim_column((FBC + 1) * odd), (row, near)),
+        )
+
+    early = outgoing(lambda r: p_hbm.at[r], lambda c: p_hbm.at[:, c])
+    loaded = outgoing(lambda r: p_v.at[1 + r, pl.ds(1, FBC)], lambda c: rim_column(1 + c))
+    up, down, across, beside = loaded
     up_in = halo(0, p_hbm.at[0], rim_below, (row - 1, col))
     down_in = halo(1, p_hbm.at[0], rim_above, (row + 1, col))
     across_in = halo(2, p_hbm.at[:, 0], rim_column((FBC + 1) * odd), (row, far))
     beside_in = halo(3, p_hbm.at[:, 0], rim_column((FBC + 1) * (1 - odd)), (row, near))
 
-    def meet():
+    def meet(copies):
+        up, down, across, beside = copies
         count = 1 - odd + has_above.astype(jnp.int32) + has_below.astype(jnp.int32) + has_far.astype(jnp.int32)
         pl.semaphore_wait(barrier, count)
+        pl.when(has_above)(up.start)
+        pl.when(has_below)(down.start)
         greet((row, near))
         pl.when(has_far)(across.start)
-        pl.when(has_above)(up.start)
-        pl.when(has_below)(down.start)
         pl.when(odd == 0)(beside.start)
 
-    pl.when(row != 1)(meet)
+    pl.when(row != 1)(lambda: meet(early))
 
     @pl.when(jnp.logical_not(has_above))
     def _():
@@ -98,6 +106,37 @@
         fill.start()
 
     chain[0] = jnp.zeros((B, 3 * B), F32)
+    first, final = 0, FBR - 1
+    inner = range(1, FBR - 1)
+
+    def column(c, rows=range(FBR)):
+        return [(r, c) for r in rows]
+
+    def end_of(r):
+        return [(r, c) for c in range(FBC)]
+
+    even_blocks = column(0, inner) + column(1, inner) + column(2, inner) + end_of(first) + end_of(final)
+    odd_blocks = column(1, inner) + column(2, inner) + column(1, (first, final)) + column(2, (first, final)) + column(0)
+    newest = 1 + FBR * FBC * KP
+
+    def find_places(blocks):
+        last = [jnp.int32(0)] * 6
+        for r, c in blocks:
+            for p in range(KP):
+                label = slot[r, c, p, p, SELF] - (col - 1) * CTD
+                at = 1 + (r * FBC + c) * KP + p
+                place = jnp.int32(0)
+                for n in range(6):
+                    place = jnp.where(label == 3 * n, last[n], place)
+                    last[n] = jnp.where(label == 3 * n, at, last[n])
+                before[at] = place
+        for n in range(6):
+            before[newest + n] = last[n]
+
+    load_slot.wait()
+    pl.when(odd == 0)(lambda: find_places(even_blocks))
+    pl.when(odd == 1)(lambda: find_places(odd_blocks))
+
     def transpose_row(r, carry):
         load_p(r).wait()
         for c in range(FBC):
@@ -106,7 +145,6 @@
         return carry
 
     lax.fori_loop(0, FBR, transpose_row, 0)
-    load_slot.wait()
 
     def products(r, c, k, rim_r, rim_c):
         right = jnp.concatenate([p_v[rim_r, rim_c, 0], p_v[rim_r, rim_c, 1]], axis=1)
@@ -134,19 +172,13 @@
         for n in range(5):
             acc[r, c, n] = sums[n]
 
-    def gather(r, c, sums, last):
+    def gather(r, c, sums):
         for p in range(KP):
             first, second = sums[1 + 2 * p], sums[2 + 2 * p]
             kinds = jnp.concatenate([first, second, sums[0] - first - second], axis=1).astype(BF16)
             term = jnp.dot(pt[r, c, p], kinds, preferred_element_type=F32)
-            label = slot[r, c, p, p, SELF] - (col - 1) * CTD
             at = 1 + (r * FBC + c) * KP + p
-            before = jnp.int32(0)
-            for n in range(6):
-                before = jnp.where(label == 3 * n, last[n], before)
-            last = [jnp.where(label == 3 * n, at, last[n]) for n in range(6)]
-            chain[at] = term + chain[before]
-        return last
+            chain[at] = term + chain[before[at]]
 
     def interior(r, verticals):
         load_a(r).wait()
@@ -169,11 +201,8 @@
         return carry
 
     lax.fori_loop(1, FBR - 1, inner_interior, 0)
-    pl.when(row == 1)(meet)
+    pl.when(row == 1)(lambda: meet(loaded))
     lax.fori_loop(0, 2, outer_interior, 0)
-
-    first, final = 0, FBR - 1
-    inner = range(1, FBR - 1)
 
     def with_side(r, c):
         k, rim = (LEFT, 0) if c == 0 else (RIGHT, FBC + 1)
@@ -187,13 +216,9 @@
         for r, c in blocks:
             hold(r, c, sums_of(r, c))
 
-    def gather_all(sums_of, blocks, last):
+    def gather_all(sums_of, blocks):
         for r, c in blocks:
-            last = gather(r, c, sums_of(r, c), last)
-        return last
-
-    def column(c, rows=range(FBR)):
-        return [(r, c) for r in rows]
+            gather(r, c, sums_of(r, c))
 
     def far_side(c):
         @pl.when(has_far)
@@ -201,40 +226,40 @@
             across_in.wait_recv()
             hold_all(with_side, column(c))
 
-    def even_order(last):
+    def even_order():
         far_side(0)
-        last = gather_all(held, column(0, inner) + column(1, inner), last)
+        gather_all(held, column(0, inner) + column(1, inner))
         beside_in.wait_recv()
         hold_all(with_side, column(2, (first, final)))
-        last = gather_all(with_side, column(2, inner), last)
+        gather_all(with_side, column(2, inner))
 
         @pl.when(has_above)
         def _():
             down_in.wait_recv()
-            hold_all(with_end, [(first, c) for c in range(FBC)])
-
-        last = gather_all(held, [(first, c) for c in range(FBC)], last)
+            hold_all(with_end, end_of(first))
+
+        gather_all(held, end_of(first))
         pl.when(has_below)(up_in.wait_recv)
-        return gather_all(with_end, [(final, c) for c in range(FBC)], last)
-
-    def odd_order(last):
+        gather_all(with_end, end_of(final))
+
+    def odd_order():
         far_side(2)
-        last = gather_all(held, column(1, inner) + column(2, inner), last)
+        gather_all(held, column(1, inner) + column(2, inner))
         pl.semaphore_wait(barrier, 1)
         beside.start()
         pl.when(has_above)(down_in.wait_recv)
         pl.when(has_below)(up_in.wait_recv)
         hold_all(with_end, [(first, 0), (final, 0)])
-        last = gather_all(with_end, [(r, c) for c in (1, 2) for r in (first, final)], last)
-
+        gather_all(with_end, column(1, (first, final)) + column(2, (first, final)))
         beside_in.wait_recv()
-        return gather_all(with_side, column(0), last)
-
-    last = lax.cond(odd == 1, odd_order, even_order, [jnp.int32(0)] * 6)
+        gather_all(with_side, column(0))
+
+    pl.when(odd == 0)(even_order)
+    pl.when(odd == 1)(odd_order)
 
     def partial_tiles(owner, target):
         for aggregate in range(2):
-            total = chain[jnp.where(owner == -1, last[aggregate], jnp.where(owner == 0, last[2 + aggregate], last[4 + aggregate]))]
+            total = chain[jnp.where(owner == -1, before[newest + aggregate], jnp.where(owner == 0, before[newest + 2 + aggregate], before[newest + 4 + aggregate]))]
             for kind in range(3):
                 target[3 * aggregate + kind] = total[:, kind * B : (kind + 1) * B].astype(target.dtype)
 
@@ -280,6 +305,7 @@
         out_specs=[pl.BlockSpec(memory_space=pltpu.VMEM), any_space, any_space],
         scratch_shapes=[
             pltpu.SMEM((FBR, FBC, KP, KP, 5), jnp.int32),
+            pltpu.SMEM((7 + FBR * FBC * KP,), jnp.int32),
             pltpu.VMEM((FBR, FBC, 5, B, B), BF16),
             pltpu.VMEM((FBR + 2, FBC + 2, KP, B, B), BF16),
             pltpu.VMEM((FBR, FBC, 5, B, B), F32),

time: 23.7 us -> 23.5 us (level)
  no operation moved by 1% of the time
where the time goes in v4:
time: 23.5 us; the launch traced here: 23.4 us
  Pallas kernels  22.6 us (96%)
  other arithmetic  0.8 us (3%)
    pallas_call x1, Pallas kernels, body(): pl.pallas_call(functools.partial(kernel, n_row, n_col), out_shape=[jax.Sh...  22.6 us
    add x1, other arithmetic, body(): return mine + far.astype(F32) + near.astype(F32)  0.8 us

profile of v4, /device:TPU:1, one launch (start us, length us, event | category | flops | bytes accessed | tf_op | source)
XLA Modules:
  0.0 23.4 jit_solution(3519135272442629250)
XLA Ops:
  0.0 22.6 %coarse.1 = (f32[6,128,128]{2,1,0:T(8,128)S(1)}, bf16[6,128,128]{2,1,0:T(8,128)(2,1)S(1)}, bf16[6,128,128]{2,1,0:T(8,128)(2,1)S(1)}) custom-call(bf16[4,3,5,128,128]{4,3,2,1,0:T(8,128)(2,1)} %a_hbm.1, bf16[4,3,2,128,128]{4,3,2,1,0:T(8,128)(2,1)} %p_hbm.1, s32[4,3,2,2,5]{4,3,2,1,0:T(2,128)} %bitcast.1), custom_call_target="tpu_custom_call" | custom-call | tf_op jit(solution)/shard_map/coarse/pallas_call | solution.py:297
  22.6 0.8 %convert_add_fusion = f32[6,128,128]{2,1,0:T(8,128)} fusion(bf16[6,128,128]{2,1,0:T(8,128)(2,1)S(1)} %get-tuple-element.10, f32[6,128,128]{2,1,0:T(8,128)S(1)} %get-tuple-element.8, bf16[6,128,128]{2,1,0:T(8,128)(2,1)S(1)} %get-tuple-element.9), kind=kLoop, calls=%fused_computation | loop fusion | flops 393216 | bytes 1179648 | tf_op jit(solution)/shard_map/add | solution.py:326

commit v5 on v4

--- a/solution.py
+++ b/solution.py
@@ -45,7 +45,7 @@
 
     for r in range(FBR):
         load_p(r).start()
-    for r in (1, 2, 0, 3):
+    for r in (1, 2):
         load_a(r).start()
 
     def halo(index, source, target, there):
@@ -145,6 +145,8 @@
         return carry
 
     lax.fori_loop(0, FBR, transpose_row, 0)
+    for r in (0, FBR - 1):
+        load_a(r).start()
 
     def products(r, c, k, rim_r, rim_c):
         right = jnp.concatenate([p_v[rim_r, rim_c, 0], p_v[rim_r, rim_c, 1]], axis=1)

time: 23.5 us -> 23.5 us (level)
  no operation moved by 1% of the time
where the time goes in v5:
time: 23.5 us; the launch traced here: 23.4 us
  Pallas kernels  22.6 us (96%)
  other arithmetic  0.8 us (3%)
    pallas_call x1, Pallas kernels, body(): pl.pallas_call(functools.partial(kernel, n_row, n_col), out_shape=[jax.Sh...  22.6 us
    add x1, other arithmetic, body(): return mine + far.astype(F32) + near.astype(F32)  0.8 us

profile of v5, /device:TPU:1, one launch (start us, length us, event | category | flops | bytes accessed | tf_op | source)
XLA Modules:
  0.0 23.4 jit_solution(16202619441369439419)
XLA Ops:
  0.0 22.6 %coarse.1 = (f32[6,128,128]{2,1,0:T(8,128)S(1)}, bf16[6,128,128]{2,1,0:T(8,128)(2,1)S(1)}, bf16[6,128,128]{2,1,0:T(8,128)(2,1)S(1)}) custom-call(bf16[4,3,5,128,128]{4,3,2,1,0:T(8,128)(2,1)} %a_hbm.1, bf16[4,3,2,128,128]{4,3,2,1,0:T(8,128)(2,1)} %p_hbm.1, s32[4,3,2,2,5]{4,3,2,1,0:T(2,128)} %bitcast.1), custom_call_target="tpu_custom_call" | custom-call | tf_op jit(solution)/shard_map/coarse/pallas_call | solution.py:299
  22.6 0.8 %convert_add_fusion = f32[6,128,128]{2,1,0:T(8,128)} fusion(bf16[6,128,128]{2,1,0:T(8,128)(2,1)S(1)} %get-tuple-element.10, f32[6,128,128]{2,1,0:T(8,128)S(1)} %get-tuple-element.8, bf16[6,128,128]{2,1,0:T(8,128)(2,1)S(1)} %get-tuple-element.9), kind=kLoop, calls=%fused_computation | loop fusion | flops 393216 | bytes 1179648 | tf_op jit(solution)/shard_map/add | solution.py:328
